TPU v7x, 512 devices: a whole 4x8x8 slice. The times are simulated.
512 devices in a mesh: grp: 8 (over y), slot: 64 (over x, z, core).
Axes of the slice: x: 4, y: 8, z: 8, core: 2. Of those that a mesh axis runs over, the one named last changes fastest.
Arguments:
- propagators: float32 [1024, 2, 128, 128], P(('grp', 'slot')), may hold values from -1 to 1, as said below
Outputs:
- forward: float32 [1024, 2, 128, 128], P(('grp', 'slot'))
Inputs may be any that keep to these rules, and one draw needn't show every extreme that they name: `propagators`: each slice is a unitary matrix of order 128, given as real and imaginary parts.
All inputs are finite; a program needn't handle non-finite values.
Results may differ from a plain program's by a relative error of at most 0.0003.
Values sent between devices are 32-bit elements; how exact they have to be, the bound alone decides.
No kernel may reach another device: no remote copies, remote signals or barrier semaphores. Data moves between devices by JAX's collectives and lax.ppermute only.
A program may use at most 64 MiB of HBM per device.

v0:
```python
import functools
import math

import jax
import jax.numpy as jnp
import numpy as np
from jax import lax
from jax.experimental import pallas as pl
from jax.experimental.pallas import tpu as pltpu
from jax.sharding import Mesh, PartitionSpec as P

VMEM = pltpu.VMEM
F32 = jnp.float32

EIGHT = ([(0, 1), (2, 3), (4, 5), (6, 7)], [(1, 2), (0, 3), (5, 6), (4, 7)], [(0, 6), (1, 7), (2, 4), (3, 5)])
FOUR = ([(0, 1), (2, 3)], [(0, 3), (1, 2)])
LEVELS = [(2, EIGHT[i], i) for i in range(3)] + [(1, FOUR[i], 3 + i) for i in range(2)] + [(0, EIGHT[i], 5 + i) for i in range(3)]


def pairs_along(ids, axis, pairs):
    lines = np.moveaxis(ids, axis, -1).reshape(-1, ids.shape[axis])
    return [[int(line[a]), int(line[b])] for line in lines for a, b in pairs]


def split(x):
    high = x.astype(jnp.bfloat16)
    rest = x - high.astype(F32)
    mid = rest.astype(jnp.bfloat16)
    low = (rest - mid.astype(F32)).astype(jnp.bfloat16)
    return high, mid, low


def product(a, b):
    cat = jnp.concatenate
    left = [cat([cat([r, -i], 1), cat([i, r], 1)], 0) for r, i in zip(split(a[0]), split(a[1]))]
    right = [cat([r, i], 0) for r, i in zip(split(b[0]), split(b[1]))]
    dot = functools.partial(jnp.dot, preferred_element_type=F32)
    n = a[0].shape[1]
    both = cat(right[:2], 1)
    c0, c1 = dot(left[0], both), dot(left[1], both)
    small = dot(left[0], right[2]) + dot(left[2], right[0]) + c1[:, n:]
    c = small + (c0[:, n:] + c1[:, :n]) + c0[:, :n]
    return c[:n], c[n:]


def load(ref, *i):
    return ref[(*i, 0)], ref[(*i, 1)]


def store(ref, c, *i):
    ref[(*i, 0)] = c[0]
    ref[(*i, 1)] = c[1]


def begin(flag, u, total, inner):
    first = product(load(u, 0, 1), load(u, 0, 0))
    second = product(load(u, 1, 1), load(u, 1, 0))
    whole = product(second, first)
    store(total, whole)

    @pl.when(flag[0] == 0)
    def _():
        inner[0] = u[0, 0]
        store(inner, first, 1)

    @pl.when(flag[0] == 1)
    def _():
        store(inner, product(load(u, 1, 0), first), 0)
        store(inner, whole, 1)


def level(bit, first, last, flag, g, *refs):
    refs = list(refs)
    before = None if first else refs.pop(0)
    if not last:
        store(refs.pop(0), product(load(g, 1), load(g, 0)))
    after = refs.pop(0)
    upper = lax.rem(lax.div(flag[0], 2 << bit), 2) == 1

    @pl.when(upper)
    def _():
        if first:
            after[...] = g[0]
        else:
            store(after, product(load(before), load(g, 0)))

    @pl.when(jnp.logical_not(upper))
    def _():
        if first:
            n = g.shape[-1]
            one = lax.broadcasted_iota(jnp.int32, (n, n), 0) == lax.broadcasted_iota(jnp.int32, (n, n), 1)
            after[0] = jnp.where(one, 1.0, 0.0).astype(F32)
            after[1] = jnp.zeros((n, n), F32)
        else:
            after[...] = before[...]


def end(scale, inner, e, out):
    for j in range(2):
        c = product(load(inner, j), load(e, 1))
        store(out, (c[0] * scale, c[1] * scale), j)


def call(body, outs, *args):
    smem = pl.BlockSpec(memory_space=pltpu.SMEM)
    vmem = pl.BlockSpec(memory_space=VMEM)
    return pl.pallas_call(
        body,
        out_shape=outs,
        in_specs=[smem if a.dtype == jnp.int32 else vmem for a in args],
        out_specs=jax.tree.map(lambda _: vmem, outs),
        compiler_params=pltpu.CompilerParams(vmem_limit_bytes=16 << 20),
    )(*args)


def local(ids, u):
    n = u.shape[-1]
    scale = math.sqrt(n)
    one = jax.ShapeDtypeStruct((2, n, n), F32)
    two = jax.ShapeDtypeStruct((2, 2, n, n), F32)
    me = lax.axis_index("d").astype(jnp.int32)
    number = me.reshape(1)
    chip = [[int(a), int(b)] for a, b in ids.reshape(-1, 2)]
    both = lax.all_gather(u, "d", axis_index_groups=chip)
    total, inner = call(begin, (one, two), lax.rem(number, 2), both)
    e = None
    for k, (axis, pairs, bit) in enumerate(LEVELS):
        other = 0 if axis == 2 else 2
        groups = pairs_along(ids[..., 1], axis, pairs) + pairs_along(ids[..., 0], other, EIGHT[0])
        g = lax.all_gather(total, "d", axis_index_groups=groups)
        last = k == len(LEVELS) - 1
        body = functools.partial(level, bit, k == 0, last)
        args = (number, g) + (() if e is None else (e,))
        if last:
            (e,) = call(body, (one,), *args)
        else:
            total, e = call(body, (one, one), *args)
    e = lax.all_gather(e, "d", axis_index_groups=chip)
    return call(functools.partial(end, scale), (two,), inner, e)[0]


def solution(mesh):
    flat = Mesh(mesh.devices.reshape(-1), ("d",))
    ids = np.arange(flat.size).reshape(8, 4, 8, 2)
    return jax.shard_map(
        functools.partial(local, ids), mesh=flat, in_specs=(P("d"),), out_specs=P("d"), check_vma=False
    )
```

profile of v0, /device:TPU:79, one launch (start us, length us, event | category | flops | bytes accessed | tf_op | source)
XLA Modules:
  0.0 61.3 jit_solution(16247125194548445314)
XLA Ops:
  0.0 2.7 %all-gather = f32[4,2,128,128]{3,2,1,0:T(8,128)S(1)} all-gather(f32[2,2,128,128]{3,2,1,0:T(8,128)} %param.1), channel_id=2, replica_groups={{0,1},{2,3},{4,5},{6,7},{8,9},{10,11},{12,13},{14,15},{16,17},{18,19},{..., dimensions={0}, use_global_device_ids=true | all-gather | bytes 786432 | tf_op jit(solution)/shard_map/all_gather | solution.py:124
  2.7 1.0 %shard_map.17 = (f32[2,128,128]{2,1,0:T(8,128)S(1)}, f32[2,2,128,128]{3,2,1,0:T(8,128)S(1)}) custom-call(s32[1]{0:T(128)S(6)} %rem.18.flag, f32[2,2,2,128,128]{4,3,2,1,0:T(8,128)S(1)} %bitcast.11), custom_call_target="tpu_custom_call" | custom-call | tf_op jit(solution)/shard_map/pallas_call | solution.py:107
  3.7 4.8 %all-gather.1 = f32[4,128,128]{2,1,0:T(8,128)S(1)} all-gather(f32[2,128,128]{2,1,0:T(8,128)S(1)} %get-tuple-element.22), channel_id=3, replica_groups={{1,3},{5,7},{9,11},{13,15},{17,19},{21,23},{25,27},{29,31},{33,35},{37,..., dimensions={0}, use_global_device_ids=true | all-gather | bytes 393216 | tf_op jit(solution)/shard_map/all_gather | solution.py:130
  8.5 0.3 shard_map.18
  8.8 7.1 %all-gather.2 = f32[4,128,128]{2,1,0:T(8,128)S(1)} all-gather(f32[2,128,128]{2,1,0:T(8,128)S(1)} %get-tuple-element.23), channel_id=4, replica_groups={{3,5},{1,7},{11,13},{9,15},{19,21},{17,23},{27,29},{25,31},{35,37},{33,..., dimensions={0}, use_global_device_ids=true | all-gather | bytes 393216 | tf_op jit(solution)/shard_map/all_gather | solution.py:130
  15.9 0.3 shard_map.19
  16.2 10.5 %all-gather.3 = f32[4,128,128]{2,1,0:T(8,128)S(1)} all-gather(f32[2,128,128]{2,1,0:T(8,128)S(1)} %get-tuple-element.25), channel_id=5, replica_groups={{1,13},{3,15},{5,9},{7,11},{17,29},{19,31},{21,25},{23,27},{33,45},{35,..., dimensions={0}, use_global_device_ids=true | all-gather | bytes 393216 | tf_op jit(solution)/shard_map/all_gather | solution.py:130
  26.7 0.3 shard_map.20
  27.0 4.5 %all-gather.4 = f32[4,128,128]{2,1,0:T(8,128)S(1)} all-gather(f32[2,128,128]{2,1,0:T(8,128)S(1)} %get-tuple-element.27), channel_id=6, replica_groups={{1,17},{33,49},{3,19},{35,51},{5,21},{37,53},{7,23},{39,55},{9,25},{41,..., dimensions={0}, use_global_device_ids=true | all-gather | bytes 393216 | tf_op jit(solution)/shard_map/all_gather | solution.py:130
  31.5 0.6 %shard_map.21 = (f32[2,128,128]{2,1,0:T(8,128)S(1)}, f32[2,128,128]{2,1,0:T(8,128)S(1)}) custom-call(s32[1]{0:T(128)} %bitcast.flag, f32[2,2,128,128]{3,2,1,0:T(8,128)S(1)} %bitcast.16, f32[2,128,128]{2,1,0:T(8,128)S(1)} %get-tuple-element.28.refs_0_), custom_call_target="tpu_custom_call" | custom-call | tf_op jit(solution)/shard_map/pallas_call | solution.py:107
  32.1 5.7 %all-gather.5 = f32[4,128,128]{2,1,0:T(8,128)S(1)} all-gather(f32[2,128,128]{2,1,0:T(8,128)S(1)} %get-tuple-element.29), channel_id=7, replica_groups={{1,49},{17,33},{3,51},{19,35},{5,53},{21,37},{7,55},{23,39},{9,57},{25,..., dimensions={0}, use_global_device_ids=true | all-gather | bytes 393216 | tf_op jit(solution)/shard_map/all_gather | solution.py:130
  37.8 0.6 %shard_map.22 = (f32[2,128,128]{2,1,0:T(8,128)S(1)}, f32[2,128,128]{2,1,0:T(8,128)S(1)}) custom-call(s32[1]{0:T(128)} %bitcast.flag, f32[2,2,128,128]{3,2,1,0:T(8,128)S(1)} %bitcast.17, f32[2,128,128]{2,1,0:T(8,128)S(1)} %get-tuple-element.30.refs_0_), custom_call_target="tpu_custom_call" | custom-call | tf_op jit(solution)/shard_map/pallas_call | solution.py:107
  38.5 4.5 %all-gather.6 = f32[4,128,128]{2,1,0:T(8,128)S(1)} all-gather(f32[2,128,128]{2,1,0:T(8,128)S(1)} %get-tuple-element.31), channel_id=8, replica_groups={{1,65},{129,193},{257,321},{385,449},{3,67},{131,195},{259,323},{387,45..., dimensions={0}, use_global_device_ids=true | all-gather | bytes 393216 | tf_op jit(solution)/shard_map/all_gather | solution.py:130
  43.0 0.6 %shard_map.23 = (f32[2,128,128]{2,1,0:T(8,128)S(1)}, f32[2,128,128]{2,1,0:T(8,128)S(1)}) custom-call(s32[1]{0:T(128)} %bitcast.flag, f32[2,2,128,128]{3,2,1,0:T(8,128)S(1)} %bitcast.18, f32[2,128,128]{2,1,0:T(8,128)S(1)} %get-tuple-element.32.refs_0_), custom_call_target="tpu_custom_call" | custom-call | tf_op jit(solution)/shard_map/pallas_call | solution.py:107
  43.6 5.9 %all-gather.7 = f32[4,128,128]{2,1,0:T(8,128)S(1)} all-gather(f32[2,128,128]{2,1,0:T(8,128)S(1)} %get-tuple-element.33), channel_id=9, replica_groups={{65,129},{1,193},{321,385},{257,449},{67,131},{3,195},{323,387},{259,45..., dimensions={0}, use_global_device_ids=true | all-gather | bytes 393216 | tf_op jit(solution)/shard_map/all_gather | solution.py:130
  49.5 0.3 shard_map.24
  49.8 8.3 %all-gather.8 = f32[4,128,128]{2,1,0:T(8,128)S(1)} all-gather(f32[2,128,128]{2,1,0:T(8,128)S(1)} %get-tuple-element.35), channel_id=10, replica_groups={{1,385},{65,449},{129,257},{193,321},{3,387},{67,451},{131,259},{195,32..., dimensions={0}, use_global_device_ids=true | all-gather | bytes 393216 | tf_op jit(solution)/shard_map/all_gather | solution.py:130
  58.1 2.0 %all-gather.9 = f32[4,128,128]{2,1,0:T(8,128)S(1)} all-gather(f32[2,128,128]{2,1,0:T(8,128)S(1)} %shard_map.25), channel_id=11, replica_groups={{0,1},{2,3},{4,5},{6,7},{8,9},{10,11},{12,13},{14,15},{16,17},{18,19},{..., dimensions={0}, use_global_device_ids=true | all-gather | bytes 393216 | tf_op jit(solution)/shard_map/all_gather | solution.py:138
  60.1 1.2 %shard_map.26 = f32[2,2,128,128]{3,2,1,0:T(8,128)} custom-call(f32[2,2,128,128]{3,2,1,0:T(8,128)S(1)} %get-tuple-element.21.inner, f32[2,2,128,128]{3,2,1,0:T(8,128)S(1)} %bitcast.13), custom_call_target="tpu_custom_call" | custom-call | tf_op jit(solution)/shard_map/pallas_call | solution.py:107
  (1 shorter events, 0.0 us)
where the time goes:
time: 61.4 us; the launch traced here: 61.3 us
  blocking collectives  55.9 us (91%)
  Pallas kernels  5.28 us (9%)
    all_gather x8, blocking collectives, local(): g = lax.all_gather(total, 'd', axis_index_groups=groups)  51.2 us
    pallas_call x10, Pallas kernels, call(): pl.pallas_call(body, out_shape=outs, in_specs=[smem if a.dtype == jnp.int...  5.28 us
    all_gather x1, blocking collectives, local(): both = lax.all_gather(u, 'd', axis_index_groups=chip)  2.68 us
    all_gather x1, blocking collectives, local(): e = lax.all_gather(e, 'd', axis_index_groups=chip)  1.99 us

commit v1 on v0

v1 whole, which is shorter than its diff:
```python
import functools
import math

import jax
import jax.numpy as jnp
import numpy as np
from jax import lax
from jax.experimental import pallas as pl
from jax.experimental.pallas import tpu as pltpu
from jax.sharding import Mesh, PartitionSpec as P

F32 = jnp.float32
RING = ([(0, 1), (2, 3), (4, 5), (6, 7)], [(1, 2), (0, 3), (5, 6), (4, 7)], [(0, 7), (3, 4), (1, 6), (2, 5)])
SHORT = ([(0, 1), (2, 3)], [(0, 3), (1, 2)])


def groups_along(ids, axis, groups):
    out = []
    for core in (1, 0):
        lines = np.moveaxis(ids[..., core], axis, -1).reshape(-1, ids.shape[axis])
        out += [[int(line[i]) for i in g] for line in lines for g in groups]
    return out


def split(x):
    high = x.astype(jnp.bfloat16)
    rest = x - high.astype(F32)
    mid = rest.astype(jnp.bfloat16)
    low = (rest - mid.astype(F32)).astype(jnp.bfloat16)
    return high, mid, low


def times(lefts, right):
    cat = jnp.concatenate
    n = right[0].shape[0]
    a = split(cat([cat(left, 1) for left in lefts], 0))
    b = [cat([cat([r, i], 1), cat([-i, r], 1)], 0) for r, i in zip(split(right[0]), split(right[1]))]
    dot = functools.partial(jnp.dot, preferred_element_type=F32)
    c = dot(a[0], b[2]) + dot(a[2], b[0]) + dot(a[1], b[1])
    c = c + (dot(a[0], b[1]) + dot(a[1], b[0])) + dot(a[0], b[0])
    return [(c[k * n : (k + 1) * n, :n], c[k * n : (k + 1) * n, n:]) for k in range(len(lefts))]


def load(ref, *i):
    return ref[(*i, 0)], ref[(*i, 1)]


def store(ref, c, *i):
    ref[(*i, 0)] = c[0]
    ref[(*i, 1)] = c[1]


def where(flag, a, b):
    return tuple(jnp.where(flag, x, y) for x, y in zip(a, b))


def begin(core, u, total, inner):
    (first,) = times([load(u, 0, 1)], load(u, 0, 0))
    (second,) = times([load(u, 1, 1)], load(u, 1, 0))
    whole, third = times([second, load(u, 1, 0)], first)
    store(total, whole)
    one = core[0] == 1
    store(inner, where(one, third, load(u, 0, 0)), 0)
    store(inner, where(one, whole, first), 1)


def pair_first(upper, g, total, after):
    (whole,) = times([load(g, 1)], load(g, 0))
    store(total, whole)
    n = g.shape[-1]
    eye = lax.broadcasted_iota(jnp.int32, (n, n), 0) == lax.broadcasted_iota(jnp.int32, (n, n), 1)
    one = jnp.where(eye, 1.0, 0.0).astype(F32), jnp.zeros((n, n), F32)
    store(after, where(upper[0] == 1, load(g, 0), one))


def pair(upper, g, before, total, after):
    e = load(before)
    whole, more = times([load(g, 1), e], load(g, 0))
    store(total, whole)
    store(after, where(upper[0] == 1, more, e))


def pair_last(upper, g, before, after):
    e = load(before)
    (more,) = times([e], load(g, 0))
    store(after, where(upper[0] == 1, more, e))


def end(scale, inner, e, out):
    for j, c in enumerate(times([load(inner, 0), load(inner, 1)], load(e))):
        store(out, (c[0] * scale, c[1] * scale), j)


def call(body, outs, *args):
    smem = pl.BlockSpec(memory_space=pltpu.SMEM)
    vmem = pl.BlockSpec(memory_space=pltpu.VMEM)
    return pl.pallas_call(
        body,
        out_shape=outs,
        in_specs=[smem if a.dtype == jnp.int32 else vmem for a in args],
        out_specs=jax.tree.map(lambda _: vmem, outs),
        compiler_params=pltpu.CompilerParams(vmem_limit_bytes=16 << 20),
    )(*args)


def local(ids, u):
    n = u.shape[-1]
    one = jax.ShapeDtypeStruct((2, n, n), F32)
    two = jax.ShapeDtypeStruct((2, 2, n, n), F32)
    me = lax.axis_index("d").astype(jnp.uint32)
    core, z, x, y = me % 2, me // 2 % 8, me // 16 % 4, me // 64
    chip = [[int(a), int(b)] for a, b in ids.reshape(-1, 2)]
    flag = lambda value: value.astype(jnp.int32).reshape(1)

    def gather(value, axis, groups):
        return lax.all_gather(value, "d", axis_index_groups=groups_along(ids, axis, groups))

    def tree(total):
        total, e = call(pair_first, (one, one), flag(z % 2), gather(total, 2, RING[0]))
        for axis, place, level in ((2, z // 2, RING[1]), (2, z // 4, RING[2]), (1, x, SHORT[0]), (1, x // 2, SHORT[1]), (0, y, RING[0]), (0, y // 2, RING[1])):
            total, e = call(pair, (one, one), flag(place % 2), gather(total, axis, level), e)
        return call(pair_last, one, flag(y // 4), gather(total, 0, RING[2]), e)

    def from_core_one(e):
        return lax.all_gather(e, "d", axis_index_groups=chip)[1]

    def nothing_before(e):
        eye = jnp.eye(n, dtype=F32)
        return jnp.stack([eye, jnp.zeros_like(eye)])

    both = lax.all_gather(u, "d", axis_index_groups=chip)
    total, inner = call(begin, (one, two), flag(core), both)
    e = lax.cond(core == 1, tree, lambda total: total, total)
    e = lax.cond(me < 2, nothing_before, from_core_one, e)
    return call(functools.partial(end, math.sqrt(n)), two, inner, e)


def solution(mesh):
    flat = Mesh(mesh.devices.reshape(-1), ("d",))
    ids = np.arange(flat.size).reshape(8, 4, 8, 2)
    return jax.shard_map(
        functools.partial(local, ids), mesh=flat, in_specs=(P("d"),), out_specs=P("d"), check_vma=False
    )
```

time: 61.4 us -> 60.9 us (level)
  the two profiles are of different devices: /device:TPU:79 before, /device:TPU:7 now
where the time goes in v1:
time: 60.9 us; the launch traced here: 60.8 us
  blocking collectives  56 us (92%)
  Pallas kernels  4.6 us (8%)
    all_gather x8, blocking collectives, gather(): lax.all_gather(value, 'd', axis_index_groups=groups_along(ids, axis, grou...  51.3 us
    pallas_call x10, Pallas kernels, call(): pl.pallas_call(body, out_shape=outs, in_specs=[smem if a.dtype == jnp.int...  4.6 us
    all_gather x1, blocking collectives, local(): both = lax.all_gather(u, 'd', axis_index_groups=chip)  2.68 us
    all_gather x1, blocking collectives, from_core_one(): return lax.all_gather(e, 'd', axis_index_groups=chip)[1]  1.99 us

profile of v1, /device:TPU:7, one launch (start us, length us, event | category | flops | bytes accessed | tf_op | source)
XLA Modules:
  0.0 60.8 jit_solution(14987297157652407462)
XLA Ops:
  0.0 2.7 %all-gather.9 = f32[4,2,128,128]{3,2,1,0:T(8,128)S(1)} all-gather(f32[2,2,128,128]{3,2,1,0:T(8,128)} %param.5), channel_id=11, replica_groups={{0,1},{2,3},{4,5},{6,7},{8,9},{10,11},{12,13},{14,15},{16,17},{18,19},{..., dimensions={0}, use_global_device_ids=true | all-gather | bytes 786432 | tf_op jit(solution)/shard_map/all_gather | solution.py:131
  2.7 0.8 %shard_map.17 = (f32[2,128,128]{2,1,0:T(8,128)S(1)}, f32[2,2,128,128]{3,2,1,0:T(8,128)S(1)}) custom-call(s32[1]{0:T(128)} %bitcast.16.core, f32[2,2,2,128,128]{4,3,2,1,0:T(8,128)S(1)} %bitcast.18), custom_call_target="tpu_custom_call" | custom-call | tf_op jit(solution)/shard_map/pallas_call | solution.py:97
  3.5 54.2 %conditional.2 = (f32[2,128,128]{2,1,0:T(8,128)S(1)}) conditional(s32[]{:T(128)} %convert_element_type.67, f32[2,128,128]{2,1,0:T(8,128)S(1)} %get-tuple-element.42, (u32[]{:T(128)}, u32[]{:T(128)}, u32[]{:T(128)}, f32[2,128,128]{2,1,0:T(8,128)S(1)}, (), /*index=5*/(), (), (), u32[]{:T(128)}) %tuple.17), branch_computations={%region_0.1_spmd, %region_1.2_spmd} | conditional | flops 25 | bytes 3146004 | solution.py:133
  3.5 5.1 %all-gather = f32[4,128,128]{2,1,0:T(8,128)S(1)} all-gather(f32[2,128,128]{2,1,0:T(8,128)S(1)} %get-tuple-element.24), channel_id=2, replica_groups={{1,3},{5,7},{9,11},{13,15},{17,19},{21,23},{25,27},{29,31},{33,35},{37,..., dimensions={0}, use_global_device_ids=true | all-gather | bytes 393216 | tf_op jit(solution)/shard_map/cond/branch_1_fun/all_gather | solution.py:116
  8.6 0.3 branch_1_fun.8
  8.9 8.2 %all-gather.1 = f32[4,128,128]{2,1,0:T(8,128)S(1)} all-gather(f32[2,128,128]{2,1,0:T(8,128)S(1)} %get-tuple-element.25), channel_id=3, replica_groups={{3,5},{1,7},{11,13},{9,15},{19,21},{17,23},{27,29},{25,31},{35,37},{33,..., dimensions={0}, use_global_device_ids=true | all-gather | bytes 393216 | tf_op jit(solution)/shard_map/cond/branch_1_fun/all_gather | solution.py:116
  17.1 0.4 branch_1_fun.9
  17.5 9.3 %all-gather.2 = f32[4,128,128]{2,1,0:T(8,128)S(1)} all-gather(f32[2,128,128]{2,1,0:T(8,128)S(1)} %get-tuple-element.27), channel_id=4, replica_groups={{1,15},{7,9},{3,13},{5,11},{17,31},{23,25},{19,29},{21,27},{33,47},{39,..., dimensions={0}, use_global_device_ids=true | all-gather | bytes 393216 | tf_op jit(solution)/shard_map/cond/branch_1_fun/all_gather | solution.py:116
  26.8 0.4 branch_1_fun.10
  27.2 4.5 %all-gather.3 = f32[4,128,128]{2,1,0:T(8,128)S(1)} all-gather(f32[2,128,128]{2,1,0:T(8,128)S(1)} %get-tuple-element.29), channel_id=5, replica_groups={{1,17},{33,49},{3,19},{35,51},{5,21},{37,53},{7,23},{39,55},{9,25},{41,..., dimensions={0}, use_global_device_ids=true | all-gather | bytes 393216 | tf_op jit(solution)/shard_map/cond/branch_1_fun/all_gather | solution.py:116
  31.7 0.4 branch_1_fun.11
  32.0 5.7 %all-gather.4 = f32[4,128,128]{2,1,0:T(8,128)S(1)} all-gather(f32[2,128,128]{2,1,0:T(8,128)S(1)} %get-tuple-element.31), channel_id=6, replica_groups={{1,49},{17,33},{3,51},{19,35},{5,53},{21,37},{7,55},{23,39},{9,57},{25,..., dimensions={0}, use_global_device_ids=true | all-gather | bytes 393216 | tf_op jit(solution)/shard_map/cond/branch_1_fun/all_gather | solution.py:116
  37.7 0.4 branch_1_fun.12
  38.1 4.5 %all-gather.5 = f32[4,128,128]{2,1,0:T(8,128)S(1)} all-gather(f32[2,128,128]{2,1,0:T(8,128)S(1)} %get-tuple-element.33), channel_id=7, replica_groups={{1,65},{129,193},{257,321},{385,449},{3,67},{131,195},{259,323},{387,45..., dimensions={0}, use_global_device_ids=true | all-gather | bytes 393216 | tf_op jit(solution)/shard_map/cond/branch_1_fun/all_gather | solution.py:116
  42.6 0.4 branch_1_fun.13
  43.0 6.4 %all-gather.6 = f32[4,128,128]{2,1,0:T(8,128)S(1)} all-gather(f32[2,128,128]{2,1,0:T(8,128)S(1)} %get-tuple-element.35), channel_id=8, replica_groups={{65,129},{1,193},{321,385},{257,449},{67,131},{3,195},{323,387},{259,45..., dimensions={0}, use_global_device_ids=true | all-gather | bytes 393216 | tf_op jit(solution)/shard_map/cond/branch_1_fun/all_gather | solution.py:116
  49.4 0.4 branch_1_fun.14
  49.8 7.6 %all-gather.7 = f32[4,128,128]{2,1,0:T(8,128)S(1)} all-gather(f32[2,128,128]{2,1,0:T(8,128)S(1)} %get-tuple-element.37), channel_id=9, replica_groups={{1,449},{193,257},{65,385},{129,321},{3,451},{195,259},{67,387},{131,32..., dimensions={0}, use_global_device_ids=true | all-gather | bytes 393216 | tf_op jit(solution)/shard_map/cond/branch_1_fun/all_gather | solution.py:116
  57.4 0.3 branch_1_fun.15
  57.7 2.0 %conditional.3 = (f32[2,128,128]{2,1,0:T(8,128)S(1)}) conditional(s32[]{:T(128)} %convert_element_type.66, f32[2,128,128]{2,1,0:T(8,128)S(1)} %get-tuple-element.53, () %tuple.18), branch_computations={%region_2.3_spmd, %region_3.4_spmd} | conditional | flops 49152 | bytes 655368 | solution.py:134
  57.7 2.0 %all-gather.8 = f32[4,128,128]{2,1,0:T(8,128)S(1)} all-gather(f32[2,128,128]{2,1,0:T(8,128)S(1)} %param.2), channel_id=10, replica_groups={{0,1},{2,3},{4,5},{6,7},{8,9},{10,11},{12,13},{14,15},{16,17},{18,19},{..., dimensions={0}, use_global_device_ids=true | all-gather | bytes 393216 | tf_op jit(solution)/shard_map/cond/branch_0_fun/all_gather | solution.py:125
  59.7 1.1 %shard_map.18 = f32[2,2,128,128]{3,2,1,0:T(8,128)} custom-call(f32[2,2,128,128]{3,2,1,0:T(8,128)S(1)} %get-tuple-element.41.inner, f32[2,128,128]{2,1,0:T(8,128)S(1)} %get-tuple-element.54.e), custom_call_target="tpu_custom_call" | custom-call | tf_op jit(solution)/shard_map/pallas_call | solution.py:97
  (1 shorter events, 0.0 us)

commit v2 on v1

--- a/solution.py
+++ b/solution.py
@@ -10,7 +10,8 @@
 from jax.sharding import Mesh, PartitionSpec as P
 
 F32 = jnp.float32
-RING = ([(0, 1), (2, 3), (4, 5), (6, 7)], [(1, 2), (0, 3), (5, 6), (4, 7)], [(0, 7), (3, 4), (1, 6), (2, 5)])
+LAST = [(0, 7), (3, 4), (1, 6), (2, 5)]
+RING = ([(0, 1), (2, 3), (4, 5), (6, 7)], [(1, 2), (0, 3), (5, 6), (4, 7)], [(0, 6), (1, 7), (2, 4), (3, 5)])
 SHORT = ([(0, 1), (2, 3)], [(0, 3), (1, 2)])
 
 
@@ -30,14 +31,18 @@
     return high, mid, low
 
 
-def times(lefts, right):
+def times(lefts, right, exact=None):
     cat = jnp.concatenate
     n = right[0].shape[0]
+    rows = n * (len(lefts) if exact is None else exact)
     a = split(cat([cat(left, 1) for left in lefts], 0))
     b = [cat([cat([r, i], 1), cat([-i, r], 1)], 0) for r, i in zip(split(right[0]), split(right[1]))]
     dot = functools.partial(jnp.dot, preferred_element_type=F32)
-    c = dot(a[0], b[2]) + dot(a[2], b[0]) + dot(a[1], b[1])
-    c = c + (dot(a[0], b[1]) + dot(a[1], b[0])) + dot(a[0], b[0])
+    c = dot(a[0], b[1]) + dot(a[1], b[0])
+    if rows:
+        more = dot(a[0][:rows], b[2]) + dot(a[2][:rows], b[0]) + dot(a[1][:rows], b[1])
+        c = c + more if rows == c.shape[0] else cat([c[:rows] + more, c[rows:]], 0)
+    c = c + dot(a[0], b[0])
     return [(c[k * n : (k + 1) * n, :n], c[k * n : (k + 1) * n, n:]) for k in range(len(lefts))]
 
 
@@ -75,19 +80,19 @@
 
 def pair(upper, g, before, total, after):
     e = load(before)
-    whole, more = times([load(g, 1), e], load(g, 0))
+    whole, more = times([load(g, 1), e], load(g, 0), 1)
     store(total, whole)
     store(after, where(upper[0] == 1, more, e))
 
 
 def pair_last(upper, g, before, after):
     e = load(before)
-    (more,) = times([e], load(g, 0))
+    (more,) = times([e], load(g, 0), 0)
     store(after, where(upper[0] == 1, more, e))
 
 
 def end(scale, inner, e, out):
-    for j, c in enumerate(times([load(inner, 0), load(inner, 1)], load(e))):
+    for j, c in enumerate(times([load(inner, 0), load(inner, 1)], load(e), 0)):
         store(out, (c[0] * scale, c[1] * scale), j)
 
 
@@ -119,7 +124,7 @@
         total, e = call(pair_first, (one, one), flag(z % 2), gather(total, 2, RING[0]))
         for axis, place, level in ((2, z // 2, RING[1]), (2, z // 4, RING[2]), (1, x, SHORT[0]), (1, x // 2, SHORT[1]), (0, y, RING[0]), (0, y // 2, RING[1])):
             total, e = call(pair, (one, one), flag(place % 2), gather(total, axis, level), e)
-        return call(pair_last, one, flag(y // 4), gather(total, 0, RING[2]), e)
+        return call(pair_last, one, flag(y // 4), gather(total, 0, LAST), e)
 
     def from_core_one(e):
         return lax.all_gather(e, "d", axis_index_groups=chip)[1]

time: 60.9 us -> 59.9 us (0.984)
  the two profiles are of different devices: /device:TPU:7 before, /device:TPU:65 now
where the time goes in v2:
time: 59.9 us; the launch traced here: 59.7 us
  blocking collectives  55.3 us (92%)
  Pallas kernels  4.22 us (7%)
    all_gather x8, blocking collectives, gather(): lax.all_gather(value, 'd', axis_index_groups=groups_along(ids, axis, grou...  50.6 us
    pallas_call x10, Pallas kernels, call(): pl.pallas_call(body, out_shape=outs, in_specs=[smem if a.dtype == jnp.int...  4.22 us
    all_gather x1, blocking collectives, local(): both = lax.all_gather(u, 'd', axis_index_groups=chip)  2.68 us
    all_gather x1, blocking collectives, from_core_one(): return lax.all_gather(e, 'd', axis_index_groups=chip)[1]  1.99 us

profile of v2, /device:TPU:65, one launch (start us, length us, event | category | flops | bytes accessed | tf_op | source)
XLA Modules:
  0.0 59.7 jit_solution(9712471665321392991)
XLA Ops:
  0.0 2.7 %all-gather.9 = f32[4,2,128,128]{3,2,1,0:T(8,128)S(1)} all-gather(f32[2,2,128,128]{3,2,1,0:T(8,128)} %param.5), channel_id=11, replica_groups={{0,1},{2,3},{4,5},{6,7},{8,9},{10,11},{12,13},{14,15},{16,17},{18,19},{..., dimensions={0}, use_global_device_ids=true | all-gather | bytes 786432 | tf_op jit(solution)/shard_map/all_gather | solution.py:136
  2.7 0.8 %shard_map.17 = (f32[2,128,128]{2,1,0:T(8,128)S(1)}, f32[2,2,128,128]{3,2,1,0:T(8,128)S(1)}) custom-call(s32[1]{0:T(128)} %bitcast.16.core, f32[2,2,2,128,128]{4,3,2,1,0:T(8,128)S(1)} %bitcast.18), custom_call_target="tpu_custom_call" | custom-call | tf_op jit(solution)/shard_map/pallas_call | solution.py:102
  3.5 53.2 %conditional.2 = (f32[2,128,128]{2,1,0:T(8,128)S(1)}) conditional(s32[]{:T(128)} %convert_element_type.67, f32[2,128,128]{2,1,0:T(8,128)S(1)} %get-tuple-element.42, (u32[]{:T(128)}, u32[]{:T(128)}, u32[]{:T(128)}, f32[2,128,128]{2,1,0:T(8,128)S(1)}, (), /*index=5*/(), (), (), u32[]{:T(128)}) %tuple.17), branch_computations={%region_0.1_spmd, %region_1.2_spmd} | conditional | flops 25 | bytes 3146004 | solution.py:138
  3.5 7.8 %all-gather = f32[4,128,128]{2,1,0:T(8,128)S(1)} all-gather(f32[2,128,128]{2,1,0:T(8,128)S(1)} %get-tuple-element.24), channel_id=2, replica_groups={{1,3},{5,7},{9,11},{13,15},{17,19},{21,23},{25,27},{29,31},{33,35},{37,..., dimensions={0}, use_global_device_ids=true | all-gather | bytes 393216 | tf_op jit(solution)/shard_map/cond/branch_1_fun/all_gather | solution.py:121
  11.2 0.3 branch_1_fun.8
  11.5 4.5 %all-gather.1 = f32[4,128,128]{2,1,0:T(8,128)S(1)} all-gather(f32[2,128,128]{2,1,0:T(8,128)S(1)} %get-tuple-element.25), channel_id=3, replica_groups={{3,5},{1,7},{11,13},{9,15},{19,21},{17,23},{27,29},{25,31},{35,37},{33,..., dimensions={0}, use_global_device_ids=true | all-gather | bytes 393216 | tf_op jit(solution)/shard_map/cond/branch_1_fun/all_gather | solution.py:121
  16.0 0.3 branch_1_fun.9
  16.4 10.8 %all-gather.2 = f32[4,128,128]{2,1,0:T(8,128)S(1)} all-gather(f32[2,128,128]{2,1,0:T(8,128)S(1)} %get-tuple-element.27), channel_id=4, replica_groups={{1,13},{3,15},{5,9},{7,11},{17,29},{19,31},{21,25},{23,27},{33,45},{35,..., dimensions={0}, use_global_device_ids=true | all-gather | bytes 393216 | tf_op jit(solution)/shard_map/cond/branch_1_fun/all_gather | solution.py:121
  27.2 0.3 branch_1_fun.10
  27.5 4.5 %all-gather.3 = f32[4,128,128]{2,1,0:T(8,128)S(1)} all-gather(f32[2,128,128]{2,1,0:T(8,128)S(1)} %get-tuple-element.29), channel_id=5, replica_groups={{1,17},{33,49},{3,19},{35,51},{5,21},{37,53},{7,23},{39,55},{9,25},{41,..., dimensions={0}, use_global_device_ids=true | all-gather | bytes 393216 | tf_op jit(solution)/shard_map/cond/branch_1_fun/all_gather | solution.py:121
  32.0 0.3 branch_1_fun.11
  32.3 5.7 %all-gather.4 = f32[4,128,128]{2,1,0:T(8,128)S(1)} all-gather(f32[2,128,128]{2,1,0:T(8,128)S(1)} %get-tuple-element.31), channel_id=6, replica_groups={{1,49},{17,33},{3,51},{19,35},{5,53},{21,37},{7,55},{23,39},{9,57},{25,..., dimensions={0}, use_global_device_ids=true | all-gather | bytes 393216 | tf_op jit(solution)/shard_map/cond/branch_1_fun/all_gather | solution.py:121
  38.1 0.3 branch_1_fun.12
  38.4 4.5 %all-gather.5 = f32[4,128,128]{2,1,0:T(8,128)S(1)} all-gather(f32[2,128,128]{2,1,0:T(8,128)S(1)} %get-tuple-element.33), channel_id=7, replica_groups={{1,65},{129,193},{257,321},{385,449},{3,67},{131,195},{259,323},{387,45..., dimensions={0}, use_global_device_ids=true | all-gather | bytes 393216 | tf_op jit(solution)/shard_map/cond/branch_1_fun/all_gather | solution.py:121
  42.9 0.3 branch_1_fun.13
  43.2 6.3 %all-gather.6 = f32[4,128,128]{2,1,0:T(8,128)S(1)} all-gather(f32[2,128,128]{2,1,0:T(8,128)S(1)} %get-tuple-element.35), channel_id=8, replica_groups={{65,129},{1,193},{321,385},{257,449},{67,131},{3,195},{323,387},{259,45..., dimensions={0}, use_global_device_ids=true | all-gather | bytes 393216 | tf_op jit(solution)/shard_map/cond/branch_1_fun/all_gather | solution.py:121
  49.5 0.3 branch_1_fun.14
  49.9 6.6 %all-gather.7 = f32[4,128,128]{2,1,0:T(8,128)S(1)} all-gather(f32[2,128,128]{2,1,0:T(8,128)S(1)} %get-tuple-element.37), channel_id=9, replica_groups={{1,449},{193,257},{65,385},{129,321},{3,451},{195,259},{67,387},{131,32..., dimensions={0}, use_global_device_ids=true | all-gather | bytes 393216 | tf_op jit(solution)/shard_map/cond/branch_1_fun/all_gather | solution.py:121
  56.4 0.2 branch_1_fun.15
  56.7 2.0 %conditional.3 = (f32[2,128,128]{2,1,0:T(8,128)S(1)}) conditional(s32[]{:T(128)} %convert_element_type.66, f32[2,128,128]{2,1,0:T(8,128)S(1)} %get-tuple-element.53, () %tuple.18), branch_computations={%region_2.3_spmd, %region_3.4_spmd} | conditional | flops 49152 | bytes 655368 | solution.py:139
  56.7 2.0 %all-gather.8 = f32[4,128,128]{2,1,0:T(8,128)S(1)} all-gather(f32[2,128,128]{2,1,0:T(8,128)S(1)} %param.2), channel_id=10, replica_groups={{0,1},{2,3},{4,5},{6,7},{8,9},{10,11},{12,13},{14,15},{16,17},{18,19},{..., dimensions={0}, use_global_device_ids=true | all-gather | bytes 393216 | tf_op jit(solution)/shard_map/cond/branch_0_fun/all_gather | solution.py:130
  58.7 1.0 %shard_map.18 = f32[2,2,128,128]{3,2,1,0:T(8,128)} custom-call(f32[2,2,128,128]{3,2,1,0:T(8,128)S(1)} %get-tuple-element.41.inner, f32[2,128,128]{2,1,0:T(8,128)S(1)} %get-tuple-element.54.e), custom_call_target="tpu_custom_call" | custom-call | tf_op jit(solution)/shard_map/pallas_call | solution.py:102
  (1 shorter events, 0.0 us)

commit v3 on v2

--- a/solution.py
+++ b/solution.py
@@ -62,7 +62,7 @@
 def begin(core, u, total, inner):
     (first,) = times([load(u, 0, 1)], load(u, 0, 0))
     (second,) = times([load(u, 1, 1)], load(u, 1, 0))
-    whole, third = times([second, load(u, 1, 0)], first)
+    whole, third = times([second, load(u, 1, 0)], first, 1)
     store(total, whole)
     one = core[0] == 1
     store(inner, where(one, third, load(u, 0, 0)), 0)
@@ -78,9 +78,9 @@
     store(after, where(upper[0] == 1, load(g, 0), one))
 
 
-def pair(upper, g, before, total, after):
+def pair(exact, upper, g, before, total, after):
     e = load(before)
-    whole, more = times([load(g, 1), e], load(g, 0), 1)
+    whole, more = times([load(g, 1), e], load(g, 0), exact)
     store(total, whole)
     store(after, where(upper[0] == 1, more, e))
 
@@ -123,7 +123,7 @@
     def tree(total):
         total, e = call(pair_first, (one, one), flag(z % 2), gather(total, 2, RING[0]))
         for axis, place, level in ((2, z // 2, RING[1]), (2, z // 4, RING[2]), (1, x, SHORT[0]), (1, x // 2, SHORT[1]), (0, y, RING[0]), (0, y // 2, RING[1])):
-            total, e = call(pair, (one, one), flag(place % 2), gather(total, axis, level), e)
+            total, e = call(functools.partial(pair, int(axis != 0)), (one, one), flag(place % 2), gather(total, axis, level), e)
         return call(pair_last, one, flag(y // 4), gather(total, 0, LAST), e)
 
     def from_core_one(e):

time: 59.9 us -> 59.7 us (level)
  no operation moved by 1% of the time
where the time goes in v3:
time: 59.7 us; the launch traced here: 59.5 us
  blocking collectives  55.3 us (93%)
  Pallas kernels  4.06 us (7%)
    all_gather x8, blocking collectives, gather(): lax.all_gather(value, 'd', axis_index_groups=groups_along(ids, axis, grou...  50.6 us
    pallas_call x10, Pallas kernels, call(): pl.pallas_call(body, out_shape=outs, in_specs=[smem if a.dtype == jnp.int...  4.06 us
    all_gather x1, blocking collectives, local(): both = lax.all_gather(u, 'd', axis_index_groups=chip)  2.68 us
    all_gather x1, blocking collectives, from_core_one(): return lax.all_gather(e, 'd', axis_index_groups=chip)[1]  1.99 us

profile of v3, /device:TPU:65, one launch (start us, length us, event | category | flops | bytes accessed | tf_op | source)
XLA Modules:
  0.0 59.5 jit_solution(14811065126187422299)
XLA Ops:
  0.0 2.7 %all-gather.9 = f32[4,2,128,128]{3,2,1,0:T(8,128)S(1)} all-gather(f32[2,2,128,128]{3,2,1,0:T(8,128)} %param.5), channel_id=11, replica_groups={{0,1},{2,3},{4,5},{6,7},{8,9},{10,11},{12,13},{14,15},{16,17},{18,19},{..., dimensions={0}, use_global_device_ids=true | all-gather | bytes 786432 | tf_op jit(solution)/shard_map/all_gather | solution.py:136
  2.7 0.7 %shard_map.17 = (f32[2,128,128]{2,1,0:T(8,128)S(1)}, f32[2,2,128,128]{3,2,1,0:T(8,128)S(1)}) custom-call(s32[1]{0:T(128)} %bitcast.16.core, f32[2,2,2,128,128]{4,3,2,1,0:T(8,128)S(1)} %bitcast.18), custom_call_target="tpu_custom_call" | custom-call | tf_op jit(solution)/shard_map/pallas_call | solution.py:102
  3.4 53.1 %conditional.2 = (f32[2,128,128]{2,1,0:T(8,128)S(1)}) conditional(s32[]{:T(128)} %convert_element_type.67, f32[2,128,128]{2,1,0:T(8,128)S(1)} %get-tuple-element.42, (u32[]{:T(128)}, u32[]{:T(128)}, u32[]{:T(128)}, f32[2,128,128]{2,1,0:T(8,128)S(1)}, (), /*index=5*/(), (), (), u32[]{:T(128)}) %tuple.17), branch_computations={%region_0.1_spmd, %region_1.2_spmd} | conditional | flops 25 | bytes 3146004 | solution.py:138
  3.4 7.8 %all-gather = f32[4,128,128]{2,1,0:T(8,128)S(1)} all-gather(f32[2,128,128]{2,1,0:T(8,128)S(1)} %get-tuple-element.24), channel_id=2, replica_groups={{1,3},{5,7},{9,11},{13,15},{17,19},{21,23},{25,27},{29,31},{33,35},{37,..., dimensions={0}, use_global_device_ids=true | all-gather | bytes 393216 | tf_op jit(solution)/shard_map/cond/branch_1_fun/all_gather | solution.py:121
  11.2 0.3 branch_1_fun.8
  11.5 4.5 %all-gather.1 = f32[4,128,128]{2,1,0:T(8,128)S(1)} all-gather(f32[2,128,128]{2,1,0:T(8,128)S(1)} %get-tuple-element.25), channel_id=3, replica_groups={{3,5},{1,7},{11,13},{9,15},{19,21},{17,23},{27,29},{25,31},{35,37},{33,..., dimensions={0}, use_global_device_ids=true | all-gather | bytes 393216 | tf_op jit(solution)/shard_map/cond/branch_1_fun/all_gather | solution.py:121
  16.0 0.3 branch_1_fun.9
  16.3 10.8 %all-gather.2 = f32[4,128,128]{2,1,0:T(8,128)S(1)} all-gather(f32[2,128,128]{2,1,0:T(8,128)S(1)} %get-tuple-element.27), channel_id=4, replica_groups={{1,13},{3,15},{5,9},{7,11},{17,29},{19,31},{21,25},{23,27},{33,45},{35,..., dimensions={0}, use_global_device_ids=true | all-gather | bytes 393216 | tf_op jit(solution)/shard_map/cond/branch_1_fun/all_gather | solution.py:121
  27.1 0.3 branch_1_fun.10
  27.5 4.5 %all-gather.3 = f32[4,128,128]{2,1,0:T(8,128)S(1)} all-gather(f32[2,128,128]{2,1,0:T(8,128)S(1)} %get-tuple-element.29), channel_id=5, replica_groups={{1,17},{33,49},{3,19},{35,51},{5,21},{37,53},{7,23},{39,55},{9,25},{41,..., dimensions={0}, use_global_device_ids=true | all-gather | bytes 393216 | tf_op jit(solution)/shard_map/cond/branch_1_fun/all_gather | solution.py:121
  32.0 0.3 branch_1_fun.11
  32.3 5.7 %all-gather.4 = f32[4,128,128]{2,1,0:T(8,128)S(1)} all-gather(f32[2,128,128]{2,1,0:T(8,128)S(1)} %get-tuple-element.31), channel_id=6, replica_groups={{1,49},{17,33},{3,51},{19,35},{5,53},{21,37},{7,55},{23,39},{9,57},{25,..., dimensions={0}, use_global_device_ids=true | all-gather | bytes 393216 | tf_op jit(solution)/shard_map/cond/branch_1_fun/all_gather | solution.py:121
  38.0 0.3 branch_1_fun.12
  38.3 4.5 %all-gather.5 = f32[4,128,128]{2,1,0:T(8,128)S(1)} all-gather(f32[2,128,128]{2,1,0:T(8,128)S(1)} %get-tuple-element.33), channel_id=7, replica_groups={{1,65},{129,193},{257,321},{385,449},{3,67},{131,195},{259,323},{387,45..., dimensions={0}, use_global_device_ids=true | all-gather | bytes 393216 | tf_op jit(solution)/shard_map/cond/branch_1_fun/all_gather | solution.py:121
  42.8 0.3 branch_1_fun.13
  43.1 6.3 %all-gather.6 = f32[4,128,128]{2,1,0:T(8,128)S(1)} all-gather(f32[2,128,128]{2,1,0:T(8,128)S(1)} %get-tuple-element.35), channel_id=8, replica_groups={{65,129},{1,193},{321,385},{257,449},{67,131},{3,195},{323,387},{259,45..., dimensions={0}, use_global_device_ids=true | all-gather | bytes 393216 | tf_op jit(solution)/shard_map/cond/branch_1_fun/all_gather | solution.py:121
  49.4 0.3 branch_1_fun.14
  49.7 6.6 %all-gather.7 = f32[4,128,128]{2,1,0:T(8,128)S(1)} all-gather(f32[2,128,128]{2,1,0:T(8,128)S(1)} %get-tuple-element.37), channel_id=9, replica_groups={{1,449},{193,257},{65,385},{129,321},{3,451},{195,259},{67,387},{131,32..., dimensions={0}, use_global_device_ids=true | all-gather | bytes 393216 | tf_op jit(solution)/shard_map/cond/branch_1_fun/all_gather | solution.py:121
  56.3 0.2 branch_1_fun.15
  56.5 2.0 %conditional.3 = (f32[2,128,128]{2,1,0:T(8,128)S(1)}) conditional(s32[]{:T(128)} %convert_element_type.66, f32[2,128,128]{2,1,0:T(8,128)S(1)} %get-tuple-element.53, () %tuple.18), branch_computations={%region_2.3_spmd, %region_3.4_spmd} | conditional | flops 49152 | bytes 655368 | solution.py:139
  56.5 2.0 %all-gather.8 = f32[4,128,128]{2,1,0:T(8,128)S(1)} all-gather(f32[2,128,128]{2,1,0:T(8,128)S(1)} %param.2), channel_id=10, replica_groups={{0,1},{2,3},{4,5},{6,7},{8,9},{10,11},{12,13},{14,15},{16,17},{18,19},{..., dimensions={0}, use_global_device_ids=true | all-gather | bytes 393216 | tf_op jit(solution)/shard_map/cond/branch_0_fun/all_gather | solution.py:130
  58.5 1.0 %shard_map.18 = f32[2,2,128,128]{3,2,1,0:T(8,128)} custom-call(f32[2,2,128,128]{3,2,1,0:T(8,128)S(1)} %get-tuple-element.41.inner, f32[2,128,128]{2,1,0:T(8,128)S(1)} %get-tuple-element.54.e), custom_call_target="tpu_custom_call" | custom-call | tf_op jit(solution)/shard_map/pallas_call | solution.py:102
  (1 shorter events, 0.0 us)

commit v4 on v3

--- a/solution.py
+++ b/solution.py
@@ -86,9 +86,13 @@
 
 
 def pair_last(upper, g, before, after):
-    e = load(before)
-    (more,) = times([e], load(g, 0), 0)
-    store(after, where(upper[0] == 1, more, e))
+    @pl.when(upper[0] == 1)
+    def _():
+        store(after, times([load(before)], load(g, 0), 0)[0])
+
+    @pl.when(upper[0] == 0)
+    def _():
+        after[...] = before[...]
 
 
 def end(scale, inner, e, out):

time: 59.7 us -> 59.5 us (level)
  no operation moved by 1% of the time
where the time goes in v4:
time: 59.5 us; the launch traced here: 59.3 us
  blocking collectives  55.3 us (93%)
  Pallas kernels  3.85 us (6%)
    all_gather x8, blocking collectives, gather(): lax.all_gather(value, 'd', axis_index_groups=groups_along(ids, axis, grou...  50.6 us
    pallas_call x10, Pallas kernels, call(): pl.pallas_call(body, out_shape=outs, in_specs=[smem if a.dtype == jnp.int...  3.85 us
    all_gather x1, blocking collectives, local(): both = lax.all_gather(u, 'd', axis_index_groups=chip)  2.68 us
    all_gather x1, blocking collectives, from_core_one(): return lax.all_gather(e, 'd', axis_index_groups=chip)[1]  1.99 us

profile of v4, /device:TPU:65, one launch (start us, length us, event | category | flops | bytes accessed | tf_op | source)
XLA Modules:
  0.0 59.3 jit_solution(1926216815811139723)
XLA Ops:
  0.0 2.7 %all-gather.9 = f32[4,2,128,128]{3,2,1,0:T(8,128)S(1)} all-gather(f32[2,2,128,128]{3,2,1,0:T(8,128)} %param.5), channel_id=11, replica_groups={{0,1},{2,3},{4,5},{6,7},{8,9},{10,11},{12,13},{14,15},{16,17},{18,19},{..., dimensions={0}, use_global_device_ids=true | all-gather | bytes 786432 | tf_op jit(solution)/shard_map/all_gather | solution.py:140
  2.7 0.7 %shard_map.17 = (f32[2,128,128]{2,1,0:T(8,128)S(1)}, f32[2,2,128,128]{3,2,1,0:T(8,128)S(1)}) custom-call(s32[1]{0:T(128)} %bitcast.16.core, f32[2,2,2,128,128]{4,3,2,1,0:T(8,128)S(1)} %bitcast.18), custom_call_target="tpu_custom_call" | custom-call | tf_op jit(solution)/shard_map/pallas_call | solution.py:106
  3.4 52.9 %conditional.2 = (f32[2,128,128]{2,1,0:T(8,128)S(1)}) conditional(s32[]{:T(128)} %convert_element_type.67, f32[2,128,128]{2,1,0:T(8,128)S(1)} %get-tuple-element.42, (u32[]{:T(128)}, u32[]{:T(128)}, u32[]{:T(128)}, f32[2,128,128]{2,1,0:T(8,128)S(1)}, (), /*index=5*/(), (), (), u32[]{:T(128)}) %tuple.17), branch_computations={%region_0.1_spmd, %region_1.2_spmd} | conditional | flops 25 | bytes 3146004 | solution.py:142
  3.4 7.8 %all-gather = f32[4,128,128]{2,1,0:T(8,128)S(1)} all-gather(f32[2,128,128]{2,1,0:T(8,128)S(1)} %get-tuple-element.24), channel_id=2, replica_groups={{1,3},{5,7},{9,11},{13,15},{17,19},{21,23},{25,27},{29,31},{33,35},{37,..., dimensions={0}, use_global_device_ids=true | all-gather | bytes 393216 | tf_op jit(solution)/shard_map/cond/branch_1_fun/all_gather | solution.py:125
  11.2 0.3 branch_1_fun.8
  11.5 4.5 %all-gather.1 = f32[4,128,128]{2,1,0:T(8,128)S(1)} all-gather(f32[2,128,128]{2,1,0:T(8,128)S(1)} %get-tuple-element.25), channel_id=3, replica_groups={{3,5},{1,7},{11,13},{9,15},{19,21},{17,23},{27,29},{25,31},{35,37},{33,..., dimensions={0}, use_global_device_ids=true | all-gather | bytes 393216 | tf_op jit(solution)/shard_map/cond/branch_1_fun/all_gather | solution.py:125
  16.0 0.3 branch_1_fun.9
  16.3 10.8 %all-gather.2 = f32[4,128,128]{2,1,0:T(8,128)S(1)} all-gather(f32[2,128,128]{2,1,0:T(8,128)S(1)} %get-tuple-element.27), channel_id=4, replica_groups={{1,13},{3,15},{5,9},{7,11},{17,29},{19,31},{21,25},{23,27},{33,45},{35,..., dimensions={0}, use_global_device_ids=true | all-gather | bytes 393216 | tf_op jit(solution)/shard_map/cond/branch_1_fun/all_gather | solution.py:125
  27.1 0.3 branch_1_fun.10
  27.5 4.5 %all-gather.3 = f32[4,128,128]{2,1,0:T(8,128)S(1)} all-gather(f32[2,128,128]{2,1,0:T(8,128)S(1)} %get-tuple-element.29), channel_id=5, replica_groups={{1,17},{33,49},{3,19},{35,51},{5,21},{37,53},{7,23},{39,55},{9,25},{41,..., dimensions={0}, use_global_device_ids=true | all-gather | bytes 393216 | tf_op jit(solution)/shard_map/cond/branch_1_fun/all_gather | solution.py:125
  32.0 0.3 branch_1_fun.11
  32.3 5.7 %all-gather.4 = f32[4,128,128]{2,1,0:T(8,128)S(1)} all-gather(f32[2,128,128]{2,1,0:T(8,128)S(1)} %get-tuple-element.31), channel_id=6, replica_groups={{1,49},{17,33},{3,51},{19,35},{5,53},{21,37},{7,55},{23,39},{9,57},{25,..., dimensions={0}, use_global_device_ids=true | all-gather | bytes 393216 | tf_op jit(solution)/shard_map/cond/branch_1_fun/all_gather | solution.py:125
  38.0 0.3 branch_1_fun.12
  38.3 4.5 %all-gather.5 = f32[4,128,128]{2,1,0:T(8,128)S(1)} all-gather(f32[2,128,128]{2,1,0:T(8,128)S(1)} %get-tuple-element.33), channel_id=7, replica_groups={{1,65},{129,193},{257,321},{385,449},{3,67},{131,195},{259,323},{387,45..., dimensions={0}, use_global_device_ids=true | all-gather | bytes 393216 | tf_op jit(solution)/shard_map/cond/branch_1_fun/all_gather | solution.py:125
  42.8 0.3 branch_1_fun.13
  43.1 6.3 %all-gather.6 = f32[4,128,128]{2,1,0:T(8,128)S(1)} all-gather(f32[2,128,128]{2,1,0:T(8,128)S(1)} %get-tuple-element.35), channel_id=8, replica_groups={{65,129},{1,193},{321,385},{257,449},{67,131},{3,195},{323,387},{259,45..., dimensions={0}, use_global_device_ids=true | all-gather | bytes 393216 | tf_op jit(solution)/shard_map/cond/branch_1_fun/all_gather | solution.py:125
  49.4 0.3 branch_1_fun.14
  49.7 6.6 %all-gather.7 = f32[4,128,128]{2,1,0:T(8,128)S(1)} all-gather(f32[2,128,128]{2,1,0:T(8,128)S(1)} %get-tuple-element.37), channel_id=9, replica_groups={{1,449},{193,257},{65,385},{129,321},{3,451},{195,259},{67,387},{131,32..., dimensions={0}, use_global_device_ids=true | all-gather | bytes 393216 | tf_op jit(solution)/shard_map/cond/branch_1_fun/all_gather | solution.py:125
  56.3 2.0 %conditional.3 = (f32[2,128,128]{2,1,0:T(8,128)S(1)}) conditional(s32[]{:T(128)} %convert_element_type.66, f32[2,128,128]{2,1,0:T(8,128)S(1)} %get-tuple-element.53, () %tuple.18), branch_computations={%region_2.3_spmd, %region_3.4_spmd} | conditional | flops 49152 | bytes 655368 | solution.py:143
  56.3 2.0 %all-gather.8 = f32[4,128,128]{2,1,0:T(8,128)S(1)} all-gather(f32[2,128,128]{2,1,0:T(8,128)S(1)} %param.2), channel_id=10, replica_groups={{0,1},{2,3},{4,5},{6,7},{8,9},{10,11},{12,13},{14,15},{16,17},{18,19},{..., dimensions={0}, use_global_device_ids=true | all-gather | bytes 393216 | tf_op jit(solution)/shard_map/cond/branch_0_fun/all_gather | solution.py:134
  58.3 1.0 %shard_map.18 = f32[2,2,128,128]{3,2,1,0:T(8,128)} custom-call(f32[2,2,128,128]{3,2,1,0:T(8,128)S(1)} %get-tuple-element.41.inner, f32[2,128,128]{2,1,0:T(8,128)S(1)} %get-tuple-element.54.e), custom_call_target="tpu_custom_call" | custom-call | tf_op jit(solution)/shard_map/pallas_call | solution.py:106
  (2 shorter events, 0.0 us)

commit v5 on v4

--- a/solution.py
+++ b/solution.py
@@ -79,10 +79,16 @@
 
 
 def pair(exact, upper, g, before, total, after):
-    e = load(before)
-    whole, more = times([load(g, 1), e], load(g, 0), exact)
-    store(total, whole)
-    store(after, where(upper[0] == 1, more, e))
+    @pl.when(upper[0] == 1)
+    def _():
+        whole, more = times([load(g, 1), load(before)], load(g, 0), exact)
+        store(total, whole)
+        store(after, more)
+
+    @pl.when(upper[0] == 0)
+    def _():
+        store(total, times([load(g, 1)], load(g, 0), exact)[0])
+        after[...] = before[...]
 
 
 def pair_last(upper, g, before, after):

time: 59.5 us -> 59.3 us (level)
  no operation moved by 1% of the time
where the time goes in v5:
time: 59.3 us; the launch traced here: 59.1 us
  blocking collectives  55.4 us (93%)
  Pallas kernels  3.53 us (6%)
    all_gather x8, blocking collectives, gather(): lax.all_gather(value, 'd', axis_index_groups=groups_along(ids, axis, grou...  50.8 us
    pallas_call x10, Pallas kernels, call(): pl.pallas_call(body, out_shape=outs, in_specs=[smem if a.dtype == jnp.int...  3.53 us
    all_gather x1, blocking collectives, local(): both = lax.all_gather(u, 'd', axis_index_groups=chip)  2.68 us
    all_gather x1, blocking collectives, from_core_one(): return lax.all_gather(e, 'd', axis_index_groups=chip)[1]  1.99 us

profile of v5, /device:TPU:65, one launch (start us, length us, event | category | flops | bytes accessed | tf_op | source)
XLA Modules:
  0.0 59.1 jit_solution(17736373401974740697)
XLA Ops:
  0.0 2.7 %all-gather.9 = f32[4,2,128,128]{3,2,1,0:T(8,128)S(1)} all-gather(f32[2,2,128,128]{3,2,1,0:T(8,128)} %param.5), channel_id=11, replica_groups={{0,1},{2,3},{4,5},{6,7},{8,9},{10,11},{12,13},{14,15},{16,17},{18,19},{..., dimensions={0}, use_global_device_ids=true | all-gather | bytes 786432 | tf_op jit(solution)/shard_map/all_gather | solution.py:146
  2.7 0.7 %shard_map.17 = (f32[2,128,128]{2,1,0:T(8,128)S(1)}, f32[2,2,128,128]{3,2,1,0:T(8,128)S(1)}) custom-call(s32[1]{0:T(128)} %bitcast.16.core, f32[2,2,2,128,128]{4,3,2,1,0:T(8,128)S(1)} %bitcast.18), custom_call_target="tpu_custom_call" | custom-call | tf_op jit(solution)/shard_map/pallas_call | solution.py:112
  3.4 52.7 %conditional.2 = (f32[2,128,128]{2,1,0:T(8,128)S(1)}) conditional(s32[]{:T(128)} %convert_element_type.67, f32[2,128,128]{2,1,0:T(8,128)S(1)} %get-tuple-element.42, (u32[]{:T(128)}, u32[]{:T(128)}, u32[]{:T(128)}, f32[2,128,128]{2,1,0:T(8,128)S(1)}, (), /*index=5*/(), (), (), u32[]{:T(128)}) %tuple.17), branch_computations={%region_0.1_spmd, %region_1.2_spmd} | conditional | flops 25 | bytes 3146004 | solution.py:148
  3.4 7.8 %all-gather = f32[4,128,128]{2,1,0:T(8,128)S(1)} all-gather(f32[2,128,128]{2,1,0:T(8,128)S(1)} %get-tuple-element.24), channel_id=2, replica_groups={{1,3},{5,7},{9,11},{13,15},{17,19},{21,23},{25,27},{29,31},{33,35},{37,..., dimensions={0}, use_global_device_ids=true | all-gather | bytes 393216 | tf_op jit(solution)/shard_map/cond/branch_1_fun/all_gather | solution.py:131
  11.2 0.3 branch_1_fun.8
  11.5 4.5 %all-gather.1 = f32[4,128,128]{2,1,0:T(8,128)S(1)} all-gather(f32[2,128,128]{2,1,0:T(8,128)S(1)} %get-tuple-element.25), channel_id=3, replica_groups={{3,5},{1,7},{11,13},{9,15},{19,21},{17,23},{27,29},{25,31},{35,37},{33,..., dimensions={0}, use_global_device_ids=true | all-gather | bytes 393216 | tf_op jit(solution)/shard_map/cond/branch_1_fun/all_gather | solution.py:131
  16.0 0.3 branch_1_fun.9
  16.3 10.9 %all-gather.2 = f32[4,128,128]{2,1,0:T(8,128)S(1)} all-gather(f32[2,128,128]{2,1,0:T(8,128)S(1)} %get-tuple-element.27), channel_id=4, replica_groups={{1,13},{3,15},{5,9},{7,11},{17,29},{19,31},{21,25},{23,27},{33,45},{35,..., dimensions={0}, use_global_device_ids=true | all-gather | bytes 393216 | tf_op jit(solution)/shard_map/cond/branch_1_fun/all_gather | solution.py:131
  27.1 0.3 branch_1_fun.10
  27.4 4.5 %all-gather.3 = f32[4,128,128]{2,1,0:T(8,128)S(1)} all-gather(f32[2,128,128]{2,1,0:T(8,128)S(1)} %get-tuple-element.29), channel_id=5, replica_groups={{1,17},{33,49},{3,19},{35,51},{5,21},{37,53},{7,23},{39,55},{9,25},{41,..., dimensions={0}, use_global_device_ids=true | all-gather | bytes 393216 | tf_op jit(solution)/shard_map/cond/branch_1_fun/all_gather | solution.py:131
  31.9 0.3 branch_1_fun.11
  32.2 5.7 %all-gather.4 = f32[4,128,128]{2,1,0:T(8,128)S(1)} all-gather(f32[2,128,128]{2,1,0:T(8,128)S(1)} %get-tuple-element.31), channel_id=6, replica_groups={{1,49},{17,33},{3,51},{19,35},{5,53},{21,37},{7,55},{23,39},{9,57},{25,..., dimensions={0}, use_global_device_ids=true | all-gather | bytes 393216 | tf_op jit(solution)/shard_map/cond/branch_1_fun/all_gather | solution.py:131
  37.9 0.3 branch_1_fun.12
  38.2 4.5 %all-gather.5 = f32[4,128,128]{2,1,0:T(8,128)S(1)} all-gather(f32[2,128,128]{2,1,0:T(8,128)S(1)} %get-tuple-element.33), channel_id=7, replica_groups={{1,65},{129,193},{257,321},{385,449},{3,67},{131,195},{259,323},{387,45..., dimensions={0}, use_global_device_ids=true | all-gather | bytes 393216 | tf_op jit(solution)/shard_map/cond/branch_1_fun/all_gather | solution.py:131
  42.7 0.2 branch_1_fun.13
  42.9 6.3 %all-gather.6 = f32[4,128,128]{2,1,0:T(8,128)S(1)} all-gather(f32[2,128,128]{2,1,0:T(8,128)S(1)} %get-tuple-element.35), channel_id=8, replica_groups={{65,129},{1,193},{321,385},{257,449},{67,131},{3,195},{323,387},{259,45..., dimensions={0}, use_global_device_ids=true | all-gather | bytes 393216 | tf_op jit(solution)/shard_map/cond/branch_1_fun/all_gather | solution.py:131
  49.2 0.2 branch_1_fun.14
  49.4 6.7 %all-gather.7 = f32[4,128,128]{2,1,0:T(8,128)S(1)} all-gather(f32[2,128,128]{2,1,0:T(8,128)S(1)} %get-tuple-element.37), channel_id=9, replica_groups={{1,449},{193,257},{65,385},{129,321},{3,451},{195,259},{67,387},{131,32..., dimensions={0}, use_global_device_ids=true | all-gather | bytes 393216 | tf_op jit(solution)/shard_map/cond/branch_1_fun/all_gather | solution.py:131
  56.1 2.0 %conditional.3 = (f32[2,128,128]{2,1,0:T(8,128)S(1)}) conditional(s32[]{:T(128)} %convert_element_type.66, f32[2,128,128]{2,1,0:T(8,128)S(1)} %get-tuple-element.53, () %tuple.18), branch_computations={%region_2.3_spmd, %region_3.4_spmd} | conditional | flops 49152 | bytes 655368 | solution.py:149
  56.1 2.0 %all-gather.8 = f32[4,128,128]{2,1,0:T(8,128)S(1)} all-gather(f32[2,128,128]{2,1,0:T(8,128)S(1)} %param.2), channel_id=10, replica_groups={{0,1},{2,3},{4,5},{6,7},{8,9},{10,11},{12,13},{14,15},{16,17},{18,19},{..., dimensions={0}, use_global_device_ids=true | all-gather | bytes 393216 | tf_op jit(solution)/shard_map/cond/branch_0_fun/all_gather | solution.py:140
  58.1 1.0 %shard_map.18 = f32[2,2,128,128]{3,2,1,0:T(8,128)} custom-call(f32[2,2,128,128]{3,2,1,0:T(8,128)S(1)} %get-tuple-element.41.inner, f32[2,128,128]{2,1,0:T(8,128)S(1)} %get-tuple-element.54.e), custom_call_target="tpu_custom_call" | custom-call | tf_op jit(solution)/shard_map/pallas_call | solution.py:112
  (2 shorter events, 0.0 us)
